TPU v7x, 32 devices: a whole 2x2x4 slice. The times are simulated.
32 devices in a mesh: tm: 8 (over z, core), tile: 4 (over y, x).
Axes of the slice: x: 2, y: 2, z: 4, core: 2. Of those that a mesh axis runs over, the one named last changes fastest.
Arguments:
- obs_values: bfloat16 [8, 8192, 128], P('tm', 'tile'), may hold values from -6 to 6
- obs_weight: bfloat16 [8, 8192, 128], P('tm', 'tile'), may hold values from 0.19921875 to 2
- obs_count: int32 [8, 8192], P('tm', 'tile'), may hold values from 32 to 128
- dest_tile: int32 [8, 8192, 1], P('tm', 'tile'), may hold values from 0 to 3; in each aligned block of 2048 rows (0 to 2047, 2048 to 4095, ..., all dimensions but the last counted through in order) at most 1024 rows name the same one
- jac_index: int32 [8, 8192], P('tm', 'tile'), may hold values from 0 to 255
- jacobian: bfloat16 [8, 1024, 128, 128], P('tm', 'tile'), may hold values from -0.5 to 0.5
- jac_state: int32 [8, 1024], P('tm', 'tile'), may hold values from 0 to 63
- corr_blocks: bfloat16 [8, 192, 128, 128], P('tm', 'tile'), may hold values from -0.625 to 0.625
- corr_row: int32 [8, 192], P('tm', 'tile'), may hold values from 0 to 63
- corr_col: int32 [8, 192], P('tm', 'tile'), may hold values from 0 to 63
- time_coupling: bfloat16 [8, 256, 128], P('tm', 'tile'), may hold values from 0.19921875 to 0.59765625
Outputs:
- product: bfloat16 [8, 8192, 128], P('tm', 'tile')
Inputs may be any that keep to these rules, and one draw needn't show every extreme that they name: `dest_tile`: in the rows of one device, no tile is named by more than 1024 observation blocks, a bound that some block reaches.
All inputs are finite; a program needn't handle non-finite values.
Results may differ from a plain program's by a relative error of at most 0.0075.
Values may be sent and summed in bfloat16 or wider, within the bound.
A program may use at most 64 MiB of HBM per device.

v0:
```python
import jax
import jax.numpy as jnp
from jax import lax
from jax.sharding import PartitionSpec as P


def from_behind(x, axis, by):
    length = lax.axis_size(axis)
    pairs = [(i, i + by) for i in range(length) if 0 <= i + by < length]
    return lax.ppermute(x, axis, pairs)


def shards(
    obs_values,
    obs_weight,
    obs_count,
    dest_tile,
    jac_index,
    jacobian,
    jac_state,
    corr_blocks,
    corr_row,
    corr_col,
    time_coupling,
):
    obs_total = obs_values.shape[1]
    block_width = obs_values.shape[2]
    jac_total = jacobian.shape[1]
    state_total = time_coupling.shape[1]
    lane_index = lax.broadcasted_iota(jnp.int32, (obs_total, block_width), 1)
    keeping = (lane_index < obs_count[0][:, None]).astype(jnp.float32)
    weighted = (
        obs_values[0].astype(jnp.float32) * obs_weight[0].astype(jnp.float32) * keeping
    ).astype(jnp.bfloat16)
    target = dest_tile[0, :, 0]
    column = jac_index[0]
    bin_id = target * jac_total + column
    row_ids = lax.broadcasted_iota(jnp.int32, (jac_total * lax.axis_size("tile"), obs_total), 0)
    picker = (row_ids == bin_id[None, :]).astype(jnp.bfloat16)
    summed = lax.psum_scatter(
        jnp.dot(picker, weighted, preferred_element_type=jnp.float32),
        "tile",
        scatter_dimension=0,
        tiled=True,
    )
    merged = summed.astype(jnp.bfloat16)
    spread = jnp.einsum("kij,ki->kj", jacobian[0], merged, preferred_element_type=jnp.float32)
    state_ids = lax.broadcasted_iota(jnp.int32, (state_total, jac_total), 0)
    owners = state_ids == jac_state[0][None, :]
    state = jnp.dot(owners.astype(jnp.float32), spread, precision=lax.Precision.HIGHEST).astype(
        jnp.bfloat16
    )
    corr_total = corr_blocks.shape[1]
    read_ids = lax.broadcasted_iota(jnp.int32, (corr_total, state_total), 1)
    reader = (read_ids == corr_col[0][:, None]).astype(jnp.bfloat16)
    source = jnp.dot(reader, state, preferred_element_type=jnp.float32).astype(jnp.bfloat16)
    mixing = jnp.einsum("cij,cj->ci", corr_blocks[0], source, preferred_element_type=jnp.float32)
    write_ids = lax.broadcasted_iota(jnp.int32, (state_total, corr_total), 0)
    writer = (write_ids == corr_row[0][None, :]).astype(jnp.float32)
    spatial = jnp.dot(writer, mixing, precision=lax.Precision.HIGHEST).astype(jnp.bfloat16)
    coupling = time_coupling[0]
    earlier = from_behind(spatial, "tm", 1)
    later_state, later_coupling = from_behind((spatial, coupling), "tm", -1)
    coupled = (
        spatial.astype(jnp.float32)
        + coupling.astype(jnp.float32) * earlier.astype(jnp.float32)
        + later_coupling.astype(jnp.float32) * later_state.astype(jnp.float32)
    ).astype(jnp.bfloat16)
    local_state = jnp.dot(
        owners.T.astype(jnp.bfloat16), coupled, preferred_element_type=jnp.float32
    ).astype(jnp.bfloat16)
    model_obs = jnp.einsum(
        "kij,kj->ki", jacobian[0], local_state, preferred_element_type=jnp.float32
    ).astype(jnp.bfloat16)
    portion = lax.all_gather(model_obs, "tile", axis=0, tiled=True)
    columns = lax.broadcasted_iota(jnp.int32, (obs_total, portion.shape[0]), 1)
    picker = (bin_id[:, None] == columns).astype(jnp.bfloat16)
    gathered = jnp.dot(picker, portion, preferred_element_type=jnp.float32)
    return (gathered * keeping).astype(jnp.bfloat16)[None]


def solution(mesh):
    in_specs = (
        P("tm", "tile", None),
        P("tm", "tile", None),
        P("tm", "tile"),
        P("tm", "tile", None),
        P("tm", "tile"),
        P("tm", "tile", None, None),
        P("tm", "tile"),
        P("tm", "tile", None, None),
        P("tm", "tile"),
        P("tm", "tile"),
        P("tm", "tile", None),
    )
    out_specs = P("tm", "tile", None)
    return jax.shard_map(shards, mesh=mesh, in_specs=in_specs, out_specs=out_specs, check_vma=False)
```

profile of v0, /device:TPU:1, one launch (start us, length us, event | category | flops | bytes accessed | tf_op | source)
XLA Modules:
  0.0 78.3 jit_solution(4623548471953794965)
XLA Ops:
  6.5 0.0 copy-start
  6.5 0.0 copy-start.4
  6.5 0.0 reduce-scatter.2.cloned.1.call-start
  6.5 0.9 %bitcast_add_fusion = s32[1,2048]{1,0:T(1,128)S(1)} fusion(s32[1,2048]{1,0:T(1,128)} %param.15, s32[1,2048,1]{1,2,0:T(1,128)} %param.14), kind=kLoop, calls=%fused_computation.38 | loop fusion | flops 4096 | bytes 24576 | tf_op jit(solution)/shard_map/add | solution.py:37
  7.4 0.0 copy-start.7
  7.4 0.0 copy-start.5
  7.4 0.0 copy-start.2
  7.4 0.0 copy-start.1
  7.4 0.0 copy-start.3
  7.5 3.6 %fusion.5 = f32[1024,128]{1,0:T(8,128)} fusion(s32[2048]{0:T(1024)S(1)} %bitcast.51, bf16[1,2048,128]{2,1,0:T(8,128)(2,1)} %param.12, bf16[1,2048,128]{2,1,0:T(8,128)(2,1)} %param.11, s32[2048]{0:T(1024)} %bitcast.55), kind=kOutput, calls=%fused_computation.7 | convolution fusion | flops 540540928 | bytes 1589248 | tf_op jit(solution)/shard_map/dot_general | solution.py:41
  11.1 0.0 reduce-scatter.2.cloned.1.call-update
  11.1 2.0 %collective-permute-start.1 = (bf16[64,128]{1,0:T(8,128)(2,1)}, bf16[64,128]{1,0:T(8,128)(2,1)S(1)}, u32[]{:S(2)}, u32[]{:S(2)}) collective-permute-start(bf16[64,128]{1,0:T(8,128)(2,1)} %bitcast.50), channel_id=1, source_target_pairs={{4,0},{8,4},{12,8},{16,12},{20,16},{24,20},{28,24},{5,1},{9,5},{13... | collective-permute-start | bytes 49160 | tf_op jit(solution)/shard_map/ppermute | solution.py:10
  13.1 24.9 %reduce-scatter.2.cloned.1.call-done = f32[256,128]{1,0:T(8,128)} async-done(((f32[1024,128]{1,0:T(8,128)}), f32[256,128]{1,0:T(8,128)}) %reduce-scatter.2.cloned.1.call-update) | async-done | bytes 131088 | tf_op jit(solution)/shard_map/reduce_scatter | solution.py:40
  38.0 0.9 %convert_bitcast_fusion = bf16[256,128,1]{1,0,2:T(8,128)(2,1)S(1)} fusion(f32[256,128]{1,0:T(8,128)} %reduce-scatter.2.cloned.1.call-done), kind=kLoop, calls=%fused_computation.28 | loop fusion | flops 32768 | bytes 196608 | tf_op jit(solution)/shard_map/convert_element_type | solution.py:46
  38.9 0.0 copy-start.6
  39.0 5.7 %fusion.2 = f32[256,1,128]{2,1,0:T(1,128)S(1)} fusion(bf16[1,256,128,128]{3,2,1,0:T(8,128)(2,1)} %param.16, bf16[256,128,1]{1,0,2:T(8,128)(2,1)S(1)} %convert_bitcast_fusion), kind=kOutput, calls=%fused_computation.2 | convolution fusion | flops 8388608 | bytes 8585216 | tf_op jit(solution)/shard_map/kij,ki->kj/dot_general | solution.py:47
  44.6 0.0 copy-done.4
  44.6 0.2 convolution_convert_fusion.2
  44.8 0.0 copy-done.7
  44.8 0.2 fusion.14
  45.0 0.0 copy-done
  45.0 0.9 %fusion.11 = f32[48,1,128]{2,1,0:T(1,128)S(1)} fusion(bf16[1,48,128,128]{3,2,1,0:T(8,128)(2,1)S(1)} %copy-done, bf16[48,128,1]{1,0,2:T(8,128)(2,1)S(1)} %fusion.14), kind=kOutput, calls=%fused_computation.13 | convolution fusion | flops 1572864 | bytes 1609728 | tf_op jit(solution)/shard_map/cij,cj->ci/dot_general | solution.py:57
  45.9 0.0 copy-done.5
  45.9 0.2 convolution_convert_fusion.1
  46.1 2.7 %collective-permute-start.2 = (bf16[64,128]{1,0:T(8,128)(2,1)S(1)}, bf16[64,128]{1,0:T(8,128)(2,1)S(1)}, u32[]{:S(2)}, u32[]{:S(2)}) collective-permute-start(bf16[64,128]{1,0:T(8,128)(2,1)S(1)} %convolution_convert_fusion.1), channel_id=1, source_target_pairs={{4,0},{8,4},{12,8},{16,12},{20,16},{24,20},{28,24},{5,1},{9,5},{13... | collective-permute-start | bytes 49160 | tf_op jit(solution)/shard_map/ppermute | solution.py:10
  48.8 3.0 %collective-permute-start = (bf16[64,128]{1,0:T(8,128)(2,1)S(1)}, bf16[64,128]{1,0:T(8,128)(2,1)S(1)}, u32[]{:S(2)}, u32[]{:S(2)}) collective-permute-start(bf16[64,128]{1,0:T(8,128)(2,1)S(1)} %convolution_convert_fusion.1), channel_id=1, source_target_pairs={{0,4},{4,8},{8,12},{12,16},{16,20},{20,24},{24,28},{1,5},{5,9},{9,... | collective-permute-start | bytes 49160 | tf_op jit(solution)/shard_map/ppermute | solution.py:10
  51.8 0.0 copy-done.2
  51.8 0.0 copy-done.1
  51.9 0.0 collective-permute-done.1
  51.9 0.0 collective-permute-done.2
  51.9 0.8 collective-permute-done
  52.7 0.0 copy-done.3
  52.7 0.2 fusion.13
  52.9 7.8 %fusion = f32[256,1,128]{2,1,0:T(1,128)S(1)} fusion(bf16[1,256,128,128]{3,2,1,0:T(8,128)(2,1)} %param.16, bf16[256,128,1]{1,0,2:T(8,128)(2,1)S(1)} %fusion.13), kind=kOutput, calls=%fused_computation | convolution fusion | flops 8388608 | bytes 8585216 | tf_op jit(solution)/shard_map/kij,kj->ki/dot_general | solution.py:72
  60.7 7.7 %all_gather.3 = bf16[1024,128]{1,0:T(8,128)(2,1)S(1)} all-gather(bf16[256,128]{1,0:T(8,128)(2,1)S(1)} %convert_element_type.71), channel_id=1, replica_groups=mesh['tm'=8,'tile'=4] {'tile'}, dimensions={0}, use_global_device_ids=true | all-gather | bytes 327680 | tf_op jit(solution)/shard_map/all_gather | solution.py:75
  68.4 0.0 copy-done.6
  68.4 3.0 %fusion.10 = bf16[1,2048,128]{2,1,0:T(8,128)(2,1)} fusion(bf16[1024,128]{1,0:T(8,128)(2,1)S(1)} %all_gather.3, s32[2048]{0:T(1024)S(1)} %add.18, s32[2048]{0:T(1024)S(1)} %bitcast.56), kind=kOutput, calls=%fused_computation.12 | convolution fusion | flops 539754496 | bytes 802816 | tf_op jit(solution)/shard_map/dot_general | solution.py:78
  (3 shorter events, 0.0 us)
Async XLA Ops:
  6.5 38.5 %copy-start = (bf16[1,48,128,128]{3,2,1,0:T(8,128)(2,1)S(1)}, bf16[1,48,128,128]{3,2,1,0:T(8,128)(2,1)}, u32[]{:S(2)}) copy-start(bf16[1,48,128,128]{3,2,1,0:T(8,128)(2,1)} %param.18) | copy-start | bytes 4718596
  6.5 38.1 %copy-start.4 = (s32[1,256]{1,0:T(1,128)S(1)}, s32[1,256]{1,0:T(1,128)}, u32[]{:S(2)}) copy-start(s32[1,256]{1,0:T(1,128)} %param.17) | copy-start | bytes 3076
  6.5 31.5 %reduce-scatter.2.cloned.1.call-start = ((), (), s32[]{:S(2)}) async-start(), calls=%async_computation.1 | async-start | bytes 655360 | tf_op jit(solution)/shard_map/reduce_scatter | solution.py:40
  7.4 37.4 %copy-start.7 = (s32[1,48]{1,0:T(1,128)S(1)}, s32[1,48]{1,0:T(1,128)}, u32[]{:S(2)}) copy-start(s32[1,48]{1,0:T(1,128)} %param.20) | copy-start | bytes 580
  7.4 38.5 %copy-start.5 = (s32[1,48]{1,0:T(1,128)S(1)}, s32[1,48]{1,0:T(1,128)}, u32[]{:S(2)}) copy-start(s32[1,48]{1,0:T(1,128)} %param.19) | copy-start | bytes 580
  7.4 44.4 %copy-start.2 = (s32[1,2048,1]{1,2,0:T(1,128)S(1)}, s32[1,2048,1]{1,2,0:T(1,128)}, u32[]{:S(2)}) copy-start(s32[1,2048,1]{1,2,0:T(1,128)} %param.14) | copy-start | bytes 24580
  7.4 44.4 %copy-start.1 = (s32[1,2048]{1,0:T(1,128)S(1)}, s32[1,2048]{1,0:T(1,128)}, u32[]{:S(2)}) copy-start(s32[1,2048]{1,0:T(1,128)} %param.15) | copy-start | bytes 24580
  7.4 45.2 %copy-start.3 = (bf16[1,64,128]{2,1,0:T(8,128)(2,1)S(1)}, bf16[1,64,128]{2,1,0:T(8,128)(2,1)}, u32[]{:S(2)}) copy-start(bf16[1,64,128]{2,1,0:T(8,128)(2,1)} %param.21) | copy-start | bytes 49156
  11.1 40.8 %collective-permute-start.1 = (bf16[64,128]{1,0:T(8,128)(2,1)}, bf16[64,128]{1,0:T(8,128)(2,1)S(1)}, u32[]{:S(2)}, u32[]{:S(2)}) collective-permute-start(bf16[64,128]{1,0:T(8,128)(2,1)} %bitcast.50), channel_id=1, source_target_pairs={{4,0},{8,4},{12,8},{16,12},{20,16},{24,20},{28,24},{5,1},{9,5},{13... | collective-permute-start | bytes 49160 | tf_op jit(solution)/shard_map/ppermute | solution.py:10
  38.9 29.5 %copy-start.6 = (s32[1,2048]{1,0:T(1,128)S(1)}, s32[1,2048]{1,0:T(1,128)}, u32[]{:S(2)}) copy-start(s32[1,2048]{1,0:T(1,128)} %param.13) | copy-start | bytes 24580
  46.1 5.8 %collective-permute-start.2 = (bf16[64,128]{1,0:T(8,128)(2,1)S(1)}, bf16[64,128]{1,0:T(8,128)(2,1)S(1)}, u32[]{:S(2)}, u32[]{:S(2)}) collective-permute-start(bf16[64,128]{1,0:T(8,128)(2,1)S(1)} %convolution_convert_fusion.1), channel_id=1, source_target_pairs={{4,0},{8,4},{12,8},{16,12},{20,16},{24,20},{28,24},{5,1},{9,5},{13... | collective-permute-start | bytes 49160 | tf_op jit(solution)/shard_map/ppermute | solution.py:10
  48.8 3.9 %collective-permute-start = (bf16[64,128]{1,0:T(8,128)(2,1)S(1)}, bf16[64,128]{1,0:T(8,128)(2,1)S(1)}, u32[]{:S(2)}, u32[]{:S(2)}) collective-permute-start(bf16[64,128]{1,0:T(8,128)(2,1)S(1)} %convolution_convert_fusion.1), channel_id=1, source_target_pairs={{0,4},{4,8},{8,12},{12,16},{16,20},{20,24},{24,28},{1,5},{5,9},{9,... | collective-permute-start | bytes 49160 | tf_op jit(solution)/shard_map/ppermute | solution.py:10
Sparse Core Ops, SparseCore 0:
  11.2 26.7 reduce-scatter.1
where the time goes:
time: 79.7 us; the launch traced here: 78.3 us
  waiting for transfers between devices  25.7 us (32%)
  matrix products  21.7 us (27%)
  between operations  13.6 us (17%)
  blocking collectives  7.71 us (10%)
  starting transfers between devices  7.68 us (10%)
  other arithmetic  1.82 us (2%)
    reduce_scatter x1, waiting for transfers between devices, shards(): lax.psum_scatter(jnp.dot(picker, weighted, preferred_element_type=jnp.flo...  24.9 us
    dot_general x1, matrix products, shards(): jnp.einsum('kij,kj->ki', jacobian[0], local_state, preferred_element_type...  7.78 us
    all_gather x1, blocking collectives, shards(): portion = lax.all_gather(model_obs, 'tile', axis=0, tiled=True)  7.71 us
    ppermute x3, starting transfers between devices, from_behind(): return lax.ppermute(x, axis, pairs)  7.67 us
    dot_general x1, matrix products, shards(): jnp.einsum('kij,ki->kj', jacobian[0], merged, preferred_element_type=jnp....  5.66 us
    dot_general x1, matrix products, shards(): jnp.dot(picker, weighted, preferred_element_type=jnp.float32)  3.62 us
    dot_general x1, matrix products, shards(): gathered = jnp.dot(picker, portion, preferred_element_type=jnp.float32)  2.99 us
  transfers between devices with their start and end apart: 4, of which 2 were waited for; matrix products, arithmetic and copies ran while one was open for 10% of the time, Pallas kernels for 0%

commit v1 on v0

v1 whole, which is shorter than its diff:
```python
import functools

import jax
import jax.numpy as jnp
from jax import lax
from jax.experimental import pallas as pl
from jax.experimental.pallas import tpu as pltpu
from jax.sharding import PartitionSpec as P

MESH = pl.DeviceIdType.MESH
GROUP = 16
CHUNKS = 4


def kernel(
    tiles,
    windows,
    count_ref,
    target_ref,
    column_ref,
    values_ref,
    weight_ref,
    jac_hbm,
    jac_state,
    corr_hbm,
    corr_row,
    corr_col,
    coupling_ref,
    out_ref,
    jac,
    corr,
    picker,
    weighted,
    keeping,
    partial,
    arrived,
    portion,
    merged,
    state,
    coupled,
    local,
    source,
    spatial_send,
    spatial_recv,
    coupling_recv,
    jac_sem,
    corr_sem,
    sum_send,
    sum_recv,
    time_send,
    time_recv,
    image_send,
    image_recv,
):
    f32, bf16 = jnp.float32, jnp.bfloat16
    me = lax.axis_index("tile")
    now = lax.axis_index("tm")
    width = values_ref.shape[1]
    obs_rows = count_ref.shape[0]
    jac_total = merged.shape[0]
    state_total = state.shape[0]
    corr_total = corr_row.shape[1]
    has_earlier, has_later = now > 0, now < windows - 1
    peers = [lax.rem(me + step, tiles) for step in range(tiles)]

    barrier = pltpu.get_barrier_semaphore()
    for peer in peers[1:]:
        pl.semaphore_signal(barrier, inc=1, device_id={"tile": peer}, device_id_type=MESH)

    @pl.when(has_earlier)
    def _():
        pl.semaphore_signal(barrier, inc=1, device_id={"tm": now - 1}, device_id_type=MESH)

    @pl.when(has_later)
    def _():
        pl.semaphore_signal(barrier, inc=1, device_id={"tm": now + 1}, device_id_type=MESH)

    jac_part = jac.shape[0] // CHUNKS
    jac_copies = []
    for part in range(CHUNKS):
        rows = pl.ds(part * jac_part, jac_part)
        jac_copies.append(pltpu.make_async_copy(jac_hbm.at[rows], jac.at[rows], jac_sem.at[part]))
        jac_copies[-1].start()
    corr_copy = pltpu.make_async_copy(corr_hbm, corr, corr_sem)
    corr_copy.start()

    lane = lax.broadcasted_iota(jnp.int32, (width, width), 1)
    eye = lax.broadcasted_iota(jnp.int32, (width, width), 0) == lane
    ones = jnp.ones((width, width), bf16)

    def upright(ref, row):
        spread = jnp.where(eye, ref[pl.ds(row, 1), :].astype(f32), 0.0).astype(bf16)
        return jnp.dot(spread, ones, preferred_element_type=f32)

    def weigh(row, carry):
        rows = pl.ds(pl.multiple_of(row * width, width), width)
        keep = (lane.astype(f32) < upright(count_ref, row)).astype(f32)
        keeping[rows, :] = keep.astype(bf16)
        weighted[rows, :] = (
            values_ref[rows, :].astype(f32) * weight_ref[rows, :].astype(f32) * keep
        ).astype(bf16)
        return carry

    lax.fori_loop(0, obs_rows, weigh, 0, unroll=4)

    bins = lax.broadcasted_iota(jnp.int32, (jac_total, width), 0)

    def partial_sum(tile):
        def add(row, total):
            wanted = jnp.where(
                target_ref[pl.ds(row, 1), :] == tile, column_ref[pl.ds(row, 1), :], -1
            )
            pick = jnp.where(bins == wanted, 1.0, 0.0).astype(bf16)
            rows = pl.ds(pl.multiple_of(row * width, width), width)
            return total + jnp.dot(pick, weighted[rows, :], preferred_element_type=f32)

        return lax.fori_loop(0, obs_rows, add, jnp.zeros((jac_total, width), f32), unroll=4)

    pl.semaphore_wait(
        barrier,
        tiles - 1 + jnp.where(has_earlier, 1, 0) + jnp.where(has_later, 1, 0),
    )

    def coupling_copy():
        return pltpu.make_async_remote_copy(
            src_ref=coupling_ref,
            dst_ref=coupling_recv,
            send_sem=time_send.at[2],
            recv_sem=time_recv.at[2],
            device_id={"tm": now - 1},
            device_id_type=MESH,
        )

    def spatial_copy(slot, to):
        return pltpu.make_async_remote_copy(
            src_ref=spatial_send,
            dst_ref=spatial_recv.at[slot],
            send_sem=time_send.at[slot],
            recv_sem=time_recv.at[slot],
            device_id={"tm": to},
            device_id_type=MESH,
        )

    @pl.when(has_earlier)
    def _():
        coupling_copy().start()

    sum_copies = []
    for step in range(1, tiles):
        partial[step - 1] = partial_sum(peers[step]).astype(bf16)
        copy = pltpu.make_async_remote_copy(
            src_ref=partial.at[step - 1],
            dst_ref=arrived.at[step - 1],
            send_sem=sum_send.at[step - 1],
            recv_sem=sum_recv.at[step - 1],
            device_id={"tile": peers[step]},
            device_id_type=MESH,
        )
        copy.start()
        sum_copies.append(copy)
    merged[...] = partial_sum(me)

    lane_f = lane.astype(f32)

    def pick_rows(row, carry):
        rows = pl.ds(pl.multiple_of(row * width, width), width)
        column = upright(column_ref, row)
        target = upright(target_ref, row)
        for tile in range(tiles):
            wanted = jnp.where(target == float(tile), column, -1.0)
            for part in range(jac_total // width):
                start = tile * jac_total + part * width
                picker[rows, start : start + width] = jnp.where(
                    wanted == lane_f + float(part * width), 1.0, 0.0
                ).astype(bf16)
        return carry

    lax.fori_loop(0, obs_rows, pick_rows, 0)

    for step in range(1, tiles):
        sum_copies[step - 1].wait_recv()
        merged[...] += arrived[step - 1].astype(f32)
    merged[...] = merged[...].astype(bf16).astype(f32)
    for copy in jac_copies:
        copy.wait()

    state_ids = lax.broadcasted_iota(jnp.int32, (state_total, width), 0)

    def to_state(group, total):
        pieces = []
        for k in range(GROUP):
            block = group * GROUP + k
            pieces.append(
                jnp.where(
                    state_ids == jac_state[0, block], merged[pl.ds(block, 1), :], 0.0
                ).astype(bf16)
            )
        rows = pl.ds(pl.multiple_of(group * GROUP * width, GROUP * width), GROUP * width)
        return total + jnp.dot(
            jnp.concatenate(pieces, axis=1), jac[rows, :], preferred_element_type=f32
        )

    blank = jnp.zeros((state_total, width), f32)
    state[...] = (
        lax.fori_loop(0, jac_total // GROUP, to_state, blank).astype(bf16).astype(f32)
    )
    corr_copy.wait()

    def correlate(group, total):
        for k in range(8):
            block = group * 8 + k
            piece = jnp.where(
                state_ids == corr_row[0, block], state[pl.ds(corr_col[0, block], 1), :], 0.0
            ).astype(bf16)
            rows = pl.ds(pl.multiple_of(block * width, width), width)
            total = total + lax.dot_general(
                piece, corr[rows, :], (((1,), (1,)), ((), ())), preferred_element_type=f32
            )
        return total

    spatial = lax.fori_loop(0, corr_total // 8, correlate, blank).astype(bf16)
    spatial_send[...] = spatial

    @pl.when(has_later)
    def _():
        spatial_copy(0, now + 1).start()

    @pl.when(has_earlier)
    def _():
        spatial_copy(1, now - 1).start()

    @pl.when(has_earlier)
    def _():
        spatial_copy(0, now - 1).wait_recv()

    @pl.when(now == 0)
    def _():
        spatial_recv[0] = jnp.zeros((state_total, width), bf16)

    @pl.when(has_later)
    def _():
        coupling_copy().wait_recv()
        spatial_copy(1, now + 1).wait_recv()

    @pl.when(now == windows - 1)
    def _():
        spatial_recv[1] = jnp.zeros((state_total, width), bf16)
        coupling_recv[...] = jnp.zeros((state_total, width), bf16)

    coupled[...] = (
        (
            spatial.astype(f32)
            + coupling_ref[...].astype(f32) * spatial_recv[0].astype(f32)
            + coupling_recv[...].astype(f32) * spatial_recv[1].astype(f32)
        )
        .astype(bf16)
        .astype(f32)
    )

    def fetch(group, carry):
        for k in range(GROUP):
            block = group * GROUP + k
            local[pl.ds(block, 1), :] = coupled[pl.ds(jac_state[0, block], 1), :]
        return carry

    lax.fori_loop(0, jac_total // GROUP, fetch, 0)

    group_ids = lax.broadcasted_iota(jnp.int32, (GROUP, width), 0)

    def images(group, carry):
        first = pl.multiple_of(group * GROUP, GROUP)
        rows = pl.ds(pl.multiple_of(group * GROUP * width, GROUP * width), GROUP * width)
        every = lax.dot_general(
            local[pl.ds(first, GROUP), :].astype(bf16),
            jac[rows, :],
            (((1,), (1,)), ((), ())),
            preferred_element_type=f32,
        )
        own = every[:, :width]
        for k in range(1, GROUP):
            own = jnp.where(group_ids == k, every[:, k * width : (k + 1) * width], own)
        portion[pl.ds(pl.multiple_of(me * jac_total + group * GROUP, GROUP), GROUP), :] = (
            own.astype(bf16)
        )
        return carry

    image_part = jac_total // CHUNKS
    groups = image_part // GROUP

    def image_copy(part, step):
        rows = pl.ds(pl.multiple_of(me * jac_total + part * image_part, image_part), image_part)
        return pltpu.make_async_remote_copy(
            src_ref=portion.at[rows],
            dst_ref=portion.at[rows],
            send_sem=image_send.at[part, step - 1],
            recv_sem=image_recv.at[part, step - 1],
            device_id={"tile": peers[step]},
            device_id_type=MESH,
        )

    for part in range(CHUNKS):
        lax.fori_loop(part * groups, (part + 1) * groups, images, 0)
        for step in range(1, tiles):
            image_copy(part, step).start()
    for part in range(CHUNKS):
        for step in range(1, tiles):
            image_copy(part, step).wait_recv()

    out_rows = 2 * width

    def gather(row, carry):
        rows = pl.ds(pl.multiple_of(row * out_rows, out_rows), out_rows)
        gathered = jnp.dot(picker[rows, :], portion[...], preferred_element_type=f32)
        out_ref[rows, :] = (gathered * keeping[rows, :].astype(f32)).astype(bf16)
        return carry

    lax.fori_loop(0, obs_rows // 2, gather, 0)

    for copy in sum_copies:
        copy.wait_send()
    for part in range(CHUNKS):
        for step in range(1, tiles):
            image_copy(part, step).wait_send()

    @pl.when(has_later)
    def _():
        spatial_copy(0, now + 1).wait_send()

    @pl.when(has_earlier)
    def _():
        spatial_copy(1, now - 1).wait_send()
        coupling_copy().wait_send()


def shards(
    tiles,
    windows,
    obs_values,
    obs_weight,
    obs_count,
    dest_tile,
    jac_index,
    jacobian,
    jac_state,
    corr_blocks,
    corr_row,
    corr_col,
    time_coupling,
):
    f32, bf16 = jnp.float32, jnp.bfloat16
    _, obs_total, width = obs_values.shape
    jac_total = jacobian.shape[1]
    corr_total = corr_blocks.shape[1]
    state_total = time_coupling.shape[1]
    vmem = pl.BlockSpec(memory_space=pltpu.VMEM)
    smem = pl.BlockSpec(memory_space=pltpu.SMEM)
    hbm = pl.BlockSpec(memory_space=pl.ANY)
    dma = pltpu.SemaphoreType.DMA
    out = pl.pallas_call(
        functools.partial(kernel, tiles, windows),
        out_shape=jax.ShapeDtypeStruct((obs_total, width), bf16),
        in_specs=[vmem] * 5 + [hbm, smem, hbm, smem, smem, vmem],
        out_specs=vmem,
        scratch_shapes=[
            pltpu.VMEM((jac_total * width, width), bf16),
            pltpu.VMEM((corr_total * width, width), bf16),
            pltpu.VMEM((obs_total, tiles * jac_total), bf16),
            pltpu.VMEM((obs_total, width), bf16),
            pltpu.VMEM((obs_total, width), bf16),
            pltpu.VMEM((tiles - 1, jac_total, width), bf16),
            pltpu.VMEM((tiles - 1, jac_total, width), bf16),
            pltpu.VMEM((tiles * jac_total, width), bf16),
            pltpu.VMEM((jac_total, width), f32),
            pltpu.VMEM((state_total, width), f32),
            pltpu.VMEM((state_total, width), f32),
            pltpu.VMEM((jac_total, width), f32),
            pltpu.VMEM((corr_total, width), f32),
            pltpu.VMEM((state_total, width), bf16),
            pltpu.VMEM((2, state_total, width), bf16),
            pltpu.VMEM((state_total, width), bf16),
            dma((CHUNKS,)),
            dma,
            dma((tiles - 1,)),
            dma((tiles - 1,)),
            dma((3,)),
            dma((3,)),
            dma((CHUNKS, tiles - 1)),
            dma((CHUNKS, tiles - 1)),
        ],
        compiler_params=pltpu.CompilerParams(
            collective_id=0, has_side_effects=True, vmem_limit_bytes=56 * 1024 * 1024
        ),
        name="dual_space",
    )(
        obs_count.reshape(obs_total // width, width),
        dest_tile.reshape(obs_total // width, width),
        jac_index.reshape(obs_total // width, width),
        obs_values[0],
        obs_weight[0],
        jacobian.reshape(jac_total * width, width),
        jac_state,
        corr_blocks.reshape(corr_total * width, width),
        corr_row,
        corr_col,
        time_coupling[0],
    )
    return out[None]


def solution(mesh):
    in_specs = (
        P("tm", "tile", None),
        P("tm", "tile", None),
        P("tm", "tile"),
        P("tm", "tile", None),
        P("tm", "tile"),
        P("tm", "tile", None, None),
        P("tm", "tile"),
        P("tm", "tile", None, None),
        P("tm", "tile"),
        P("tm", "tile"),
        P("tm", "tile", None),
    )
    out_specs = P("tm", "tile", None)
    body = functools.partial(shards, mesh.shape["tile"], mesh.shape["tm"])
    return jax.shard_map(body, mesh=mesh, in_specs=in_specs, out_specs=out_specs, check_vma=False)
```

time: 79.7 us -> 31.8 us (0.40); the launches traced: 78.3 us -> 31.6 us
  Pallas kernels: 0 us -> 29.8 us
  waiting for transfers between devices: 25.7 us -> 0 us
  matrix products: 21.7 us -> 0 us
  between operations: 13.6 us -> 0.01 us
  blocking collectives: 7.71 us -> 0 us
  starting transfers between devices: 7.68 us -> 0 us
  local copies, waits for them, and re-layouts: 0.04 us -> 1.87 us
  other arithmetic: 1.82 us -> 0 us
    pallas_call x0 -> x1, Pallas kernels: none -> 29.8 us  [shards(): pl.pallas_call(functools.partial(kernel, tiles, windows), out_shape=jax.S...]
    reduce_scatter x1 -> x0, waiting for transfers between devices: 24.9 us -> none  [shards(): lax.psum_scatter(jnp.dot(picker, weighted, preferred_element_type=jnp.flo...]
    dot_general x9 -> x0, matrix products: 21.7 us -> none  [the longest x1 7.78 us: shards(): jnp.einsum('kij,kj->ki', jacobian[0], local_state, preferred_element_type...]
    all_gather x1 -> x0, blocking collectives: 7.71 us -> none  [shards(): portion = lax.all_gather(model_obs, 'tile', axis=0, tiled=True)]
    ppermute x3 -> x0, starting transfers between devices: 7.67 us -> none  [from_behind(): return lax.ppermute(x, axis, pairs)]
    unnamed x16 -> x1, local copies, waits for them, and re-layouts: 0.04 us -> 1.87 us
    convert_element_type x2 -> x0, other arithmetic: 0.95 us -> none  [the longest x1 0.91 us: shards(): merged = summed.astype(jnp.bfloat16)]
    add x2 -> x0, other arithmetic: 0.86 us -> none  [shards(): bin_id = target * jac_total + column]
  transfers between devices with their start and end apart: 4 -> 0, of which waited for: 2 -> 0; matrix products, arithmetic and copies ran while one was open for 10% -> 0% of each run, Pallas kernels for 0% -> 0%
where the time goes in v1:
time: 31.8 us; the launch traced here: 31.6 us
  Pallas kernels  29.8 us (94%)
  local copies, waits for them, and re-layouts  1.87 us (6%)
    pallas_call x1, Pallas kernels, shards(): pl.pallas_call(functools.partial(kernel, tiles, windows), out_shape=jax.S...  29.8 us
    unnamed x1, local copies, waits for them, and re-layouts  1.87 us

profile of v1, /device:TPU:1, one launch (start us, length us, event | category | flops | bytes accessed | tf_op | source)
XLA Modules:
  0.0 31.6 jit_solution(13474679923347952521)
XLA Ops:
  0.0 29.8 %dual_space.1 = bf16[2048,128]{1,0:T(8,128)(2,1)} custom-call(s32[16,128]{1,0:T(8,128)} %bitcast.15, s32[16,128]{1,0:T(8,128)} %bitcast.16, s32[16,128]{1,0:T(8,128)} %bitcast.17, bf16[2048,128]{1,0:T(8,128)(2,1)} %bitcast.12, bf16[2048,128]{1,0:T(8,128)(2,1)} %bitcast.13, bf16[32768,128]{1,0:T(8,128)(2,1)} %bitcast.9, s32[1,256]{1,0:T(1,128)} %jac_state.1, ...), custom_call_target="tpu_custom_call" | custom-call | tf_op jit(solution)/shard_map/dual_space/pallas_call | solution.py:359
  29.8 1.9 %copy.13 = bf16[1,2048,128]{2,1,0:T(8,128)(2,1)} copy(bf16[1,2048,128]{2,1,0:T(8,128)(2,1)} %bitcast.10) | data formatting | bytes 1048576

commit v2 on v1

--- a/solution.py
+++ b/solution.py
@@ -18,14 +18,18 @@
     count_ref,
     target_ref,
     column_ref,
-    values_ref,
-    weight_ref,
+    values_hbm,
+    weight_hbm,
     jac_hbm,
     jac_state,
     corr_hbm,
     corr_row,
     corr_col,
     coupling_ref,
+    out_hbm,
+    values_ref,
+    weight_ref,
+    picks,
     out_ref,
     jac,
     corr,
@@ -43,6 +47,8 @@
     spatial_send,
     spatial_recv,
     coupling_recv,
+    obs_sem,
+    out_sem,
     jac_sem,
     corr_sem,
     sum_send,
@@ -63,6 +69,12 @@
     has_earlier, has_later = now > 0, now < windows - 1
     peers = [lax.rem(me + step, tiles) for step in range(tiles)]
 
+    obs_copies = [
+        pltpu.make_async_copy(values_hbm, values_ref, obs_sem.at[0]),
+        pltpu.make_async_copy(weight_hbm, weight_ref, obs_sem.at[1]),
+    ]
+    for copy in obs_copies:
+        copy.start()
     barrier = pltpu.get_barrier_semaphore()
     for peer in peers[1:]:
         pl.semaphore_signal(barrier, inc=1, device_id={"tile": peer}, device_id_type=MESH)
@@ -101,20 +113,28 @@
         ).astype(bf16)
         return carry
 
-    lax.fori_loop(0, obs_rows, weigh, 0, unroll=4)
 
     bins = lax.broadcasted_iota(jnp.int32, (jac_total, width), 0)
 
-    def partial_sum(tile):
-        def add(row, total):
+    def pick_tile(tile, slot):
+        def one(row, carry):
             wanted = jnp.where(
                 target_ref[pl.ds(row, 1), :] == tile, column_ref[pl.ds(row, 1), :], -1
             )
-            pick = jnp.where(bins == wanted, 1.0, 0.0).astype(bf16)
-            rows = pl.ds(pl.multiple_of(row * width, width), width)
-            return total + jnp.dot(pick, weighted[rows, :], preferred_element_type=f32)
-
-        return lax.fori_loop(0, obs_rows, add, jnp.zeros((jac_total, width), f32), unroll=4)
+            columns = pl.ds(pl.multiple_of(row * width, width), width)
+            picks[slot, :, columns] = jnp.where(bins == wanted, 1.0, 0.0).astype(bf16)
+            return carry
+
+        lax.fori_loop(0, obs_rows, one, 0, unroll=True)
+
+    def partial_sum(slot):
+        return jnp.dot(picks[slot], weighted[...], preferred_element_type=f32)
+
+    turns = [*range(1, tiles), 0]
+    pick_tile(peers[turns[0]], 0)
+    for copy in obs_copies:
+        copy.wait()
+    lax.fori_loop(0, obs_rows, weigh, 0, unroll=True)
 
     pl.semaphore_wait(
         barrier,
@@ -146,8 +166,13 @@
         coupling_copy().start()
 
     sum_copies = []
-    for step in range(1, tiles):
-        partial[step - 1] = partial_sum(peers[step]).astype(bf16)
+    for turn, step in enumerate(turns):
+        if turn > 0:
+            pick_tile(peers[step], turn % 2)
+        if step == 0:
+            merged[...] = partial_sum(turn % 2)
+            continue
+        partial[step - 1] = partial_sum(turn % 2).astype(bf16)
         copy = pltpu.make_async_remote_copy(
             src_ref=partial.at[step - 1],
             dst_ref=arrived.at[step - 1],
@@ -158,7 +183,6 @@
         )
         copy.start()
         sum_copies.append(copy)
-    merged[...] = partial_sum(me)
 
     lane_f = lane.astype(f32)
 
@@ -175,7 +199,7 @@
                 ).astype(bf16)
         return carry
 
-    lax.fori_loop(0, obs_rows, pick_rows, 0)
+    lax.fori_loop(0, obs_rows, pick_rows, 0, unroll=2)
 
     for step in range(1, tiles):
         sum_copies[step - 1].wait_recv()
@@ -202,7 +226,7 @@
 
     blank = jnp.zeros((state_total, width), f32)
     state[...] = (
-        lax.fori_loop(0, jac_total // GROUP, to_state, blank).astype(bf16).astype(f32)
+        lax.fori_loop(0, jac_total // GROUP, to_state, blank, unroll=4).astype(bf16).astype(f32)
     )
     corr_copy.wait()
 
@@ -218,7 +242,7 @@
             )
         return total
 
-    spatial = lax.fori_loop(0, corr_total // 8, correlate, blank).astype(bf16)
+    spatial = lax.fori_loop(0, corr_total // 8, correlate, blank, unroll=True).astype(bf16)
     spatial_send[...] = spatial
 
     @pl.when(has_later)
@@ -263,7 +287,7 @@
             local[pl.ds(block, 1), :] = coupled[pl.ds(jac_state[0, block], 1), :]
         return carry
 
-    lax.fori_loop(0, jac_total // GROUP, fetch, 0)
+    lax.fori_loop(0, jac_total // GROUP, fetch, 0, unroll=True)
 
     group_ids = lax.broadcasted_iota(jnp.int32, (GROUP, width), 0)
 
@@ -299,22 +323,24 @@
         )
 
     for part in range(CHUNKS):
-        lax.fori_loop(part * groups, (part + 1) * groups, images, 0)
+        lax.fori_loop(part * groups, (part + 1) * groups, images, 0, unroll=True)
         for step in range(1, tiles):
             image_copy(part, step).start()
     for part in range(CHUNKS):
         for step in range(1, tiles):
             image_copy(part, step).wait_recv()
 
-    out_rows = 2 * width
-
-    def gather(row, carry):
-        rows = pl.ds(pl.multiple_of(row * out_rows, out_rows), out_rows)
+    out_rows = obs_rows * width // CHUNKS
+    out_copies = []
+    for part in range(CHUNKS):
+        rows = pl.ds(part * out_rows, out_rows)
         gathered = jnp.dot(picker[rows, :], portion[...], preferred_element_type=f32)
         out_ref[rows, :] = (gathered * keeping[rows, :].astype(f32)).astype(bf16)
-        return carry
-
-    lax.fori_loop(0, obs_rows // 2, gather, 0)
+        copy = pltpu.make_async_copy(out_ref.at[rows], out_hbm.at[rows], out_sem.at[part])
+        copy.start()
+        out_copies.append(copy)
+    for copy in out_copies:
+        copy.wait()
 
     for copy in sum_copies:
         copy.wait_send()
@@ -330,6 +356,17 @@
     def _():
         spatial_copy(1, now - 1).wait_send()
         coupling_copy().wait_send()
+
+
+def hand_over(held, out, sem):
+    part = held.shape[0] // CHUNKS
+    copies = []
+    for k in range(CHUNKS):
+        rows = pl.ds(k * part, part)
+        copies.append(pltpu.make_async_copy(held.at[rows], out.at[rows], sem.at[k]))
+        copies[-1].start()
+    for copy in copies:
+        copy.wait()
 
 
 def shards(
@@ -359,9 +396,13 @@
     out = pl.pallas_call(
         functools.partial(kernel, tiles, windows),
         out_shape=jax.ShapeDtypeStruct((obs_total, width), bf16),
-        in_specs=[vmem] * 5 + [hbm, smem, hbm, smem, smem, vmem],
-        out_specs=vmem,
+        in_specs=[vmem] * 3 + [hbm] * 3 + [smem, hbm, smem, smem, vmem],
+        out_specs=hbm,
         scratch_shapes=[
+            pltpu.VMEM((obs_total, width), bf16),
+            pltpu.VMEM((obs_total, width), bf16),
+            pltpu.VMEM((2, jac_total, obs_total), bf16),
+            pltpu.VMEM((obs_total, width), bf16),
             pltpu.VMEM((jac_total * width, width), bf16),
             pltpu.VMEM((corr_total * width, width), bf16),
             pltpu.VMEM((obs_total, tiles * jac_total), bf16),
@@ -378,6 +419,8 @@
             pltpu.VMEM((state_total, width), bf16),
             pltpu.VMEM((2, state_total, width), bf16),
             pltpu.VMEM((state_total, width), bf16),
+            dma((2,)),
+            dma((CHUNKS,)),
             dma((CHUNKS,)),
             dma,
             dma((tiles - 1,)),
@@ -404,6 +447,14 @@
         corr_col,
         time_coupling[0],
     )
+    out = pl.pallas_call(
+        hand_over,
+        out_shape=jax.ShapeDtypeStruct((obs_total, width), bf16),
+        in_specs=[hbm],
+        out_specs=hbm,
+        scratch_shapes=[dma((CHUNKS,))],
+        name="hand_over",
+    )(out)
     return out[None]
 
 

time: 31.8 us -> 42.2 us (1.33)
  Pallas kernels: 29.8 us -> 42 us
  local copies, waits for them, and re-layouts: 1.87 us -> 0 us
    pallas_call x0 -> x1, Pallas kernels: none -> 17 us  [shards(): pl.pallas_call(hand_over, out_shape=jax.ShapeDtypeStruct((obs_total, widt...]
    pallas_call x1, Pallas kernels: 29.8 us -> 25 us  [shards(): pl.pallas_call(functools.partial(kernel, tiles, windows), out_shape=jax.S...]
    unnamed x1 -> x0, local copies, waits for them, and re-layouts: 1.87 us -> none
where the time goes in v2:
time: 42.2 us; the launch traced here: 42 us
  Pallas kernels  42 us (100%)
    pallas_call x1, Pallas kernels, shards(): pl.pallas_call(functools.partial(kernel, tiles, windows), out_shape=jax.S...  25 us
    pallas_call x1, Pallas kernels, shards(): pl.pallas_call(hand_over, out_shape=jax.ShapeDtypeStruct((obs_total, widt...  17 us

profile of v2, /device:TPU:1, one launch (start us, length us, event | category | flops | bytes accessed | tf_op | source)
XLA Modules:
  0.0 42.0 jit_solution(18266107436464383740)
XLA Ops:
  0.0 25.0 %dual_space.1.held = bf16[2048,128]{1,0:T(8,128)(2,1)} custom-call(s32[16,128]{1,0:T(8,128)} %bitcast.14, s32[16,128]{1,0:T(8,128)} %bitcast.15, s32[16,128]{1,0:T(8,128)} %bitcast.16, bf16[2048,128]{1,0:T(8,128)(2,1)} %bitcast.11, bf16[2048,128]{1,0:T(8,128)(2,1)} %bitcast.12, bf16[32768,128]{1,0:T(8,128)(2,1)} %bitcast.9, s32[1,256]{1,0:T(1,128)} %jac_state.1, ...), custom_call_target="tpu_custom_call" | custom-call | tf_op jit(solution)/shard_map/dual_space/pallas_call | solution.py:396
  25.0 17.0 %hand_over.1 = bf16[2048,128]{1,0:T(8,128)(2,1)} custom-call(bf16[2048,128]{1,0:T(8,128)(2,1)} %dual_space.1.held), custom_call_target="tpu_custom_call" | custom-call | tf_op jit(solution)/shard_map/hand_over/pallas_call | solution.py:450

commit v3 on v2

--- a/solution.py
+++ b/solution.py
@@ -130,7 +130,7 @@
     def partial_sum(slot):
         return jnp.dot(picks[slot], weighted[...], preferred_element_type=f32)
 
-    turns = [*range(1, tiles), 0]
+    turns = sorted(range(1, tiles), key=lambda step: -abs(step - tiles // 2)) + [0]
     pick_tile(peers[turns[0]], 0)
     for copy in obs_copies:
         copy.wait()
@@ -182,7 +182,7 @@
             device_id_type=MESH,
         )
         copy.start()
-        sum_copies.append(copy)
+        sum_copies.append((step, copy))
 
     lane_f = lane.astype(f32)
 
@@ -199,10 +199,10 @@
                 ).astype(bf16)
         return carry
 
-    lax.fori_loop(0, obs_rows, pick_rows, 0, unroll=2)
-
-    for step in range(1, tiles):
-        sum_copies[step - 1].wait_recv()
+    lax.fori_loop(0, obs_rows // 2, pick_rows, 0, unroll=2)
+
+    for step, copy in sum_copies:
+        copy.wait_recv()
         merged[...] += arrived[step - 1].astype(f32)
     merged[...] = merged[...].astype(bf16).astype(f32)
     for copy in jac_copies:
@@ -253,6 +253,8 @@
     def _():
         spatial_copy(1, now - 1).start()
 
+    lax.fori_loop(obs_rows // 2, obs_rows, pick_rows, 0, unroll=2)
+
     @pl.when(has_earlier)
     def _():
         spatial_copy(0, now - 1).wait_recv()
@@ -342,7 +344,7 @@
     for copy in out_copies:
         copy.wait()
 
-    for copy in sum_copies:
+    for step, copy in sum_copies:
         copy.wait_send()
     for part in range(CHUNKS):
         for step in range(1, tiles):
@@ -358,14 +360,18 @@
         coupling_copy().wait_send()
 
 
-def hand_over(held, out, sem):
+def hand_over(held, out, stage, in_sem, out_sem):
     part = held.shape[0] // CHUNKS
-    copies = []
+    incoming, outgoing = [], []
     for k in range(CHUNKS):
         rows = pl.ds(k * part, part)
-        copies.append(pltpu.make_async_copy(held.at[rows], out.at[rows], sem.at[k]))
-        copies[-1].start()
-    for copy in copies:
+        incoming.append(pltpu.make_async_copy(held.at[rows], stage.at[rows], in_sem.at[k]))
+        outgoing.append(pltpu.make_async_copy(stage.at[rows], out.at[rows], out_sem.at[k]))
+        incoming[-1].start()
+    for k in range(CHUNKS):
+        incoming[k].wait()
+        outgoing[k].start()
+    for copy in outgoing:
         copy.wait()
 
 
@@ -452,7 +458,11 @@
         out_shape=jax.ShapeDtypeStruct((obs_total, width), bf16),
         in_specs=[hbm],
         out_specs=hbm,
-        scratch_shapes=[dma((CHUNKS,))],
+        scratch_shapes=[
+            pltpu.VMEM((obs_total, width), bf16),
+            dma((CHUNKS,)),
+            dma((CHUNKS,)),
+        ],
         name="hand_over",
     )(out)
     return out[None]

time: 42.2 us -> 26.1 us (0.62)
  Pallas kernels: 42 us -> 25.9 us
    pallas_call x1, Pallas kernels: 17 us -> 1.82 us  [shards(): pl.pallas_call(hand_over, out_shape=jax.ShapeDtypeStruct((obs_total, widt...]
    pallas_call x1, Pallas kernels: 25 us -> 24 us  [shards(): pl.pallas_call(functools.partial(kernel, tiles, windows), out_shape=jax.S...]
where the time goes in v3:
time: 26.1 us; the launch traced here: 25.9 us
  Pallas kernels  25.9 us (99%)
    pallas_call x1, Pallas kernels, shards(): pl.pallas_call(functools.partial(kernel, tiles, windows), out_shape=jax.S...  24 us
    pallas_call x1, Pallas kernels, shards(): pl.pallas_call(hand_over, out_shape=jax.ShapeDtypeStruct((obs_total, widt...  1.82 us

profile of v3, /device:TPU:1, one launch (start us, length us, event | category | flops | bytes accessed | tf_op | source)
XLA Modules:
  0.0 25.9 jit_solution(3483183798295244939)
XLA Ops:
  0.0 24.0 %dual_space.1.held = bf16[2048,128]{1,0:T(8,128)(2,1)} custom-call(s32[16,128]{1,0:T(8,128)} %bitcast.14, s32[16,128]{1,0:T(8,128)} %bitcast.15, s32[16,128]{1,0:T(8,128)} %bitcast.16, bf16[2048,128]{1,0:T(8,128)(2,1)} %bitcast.11, bf16[2048,128]{1,0:T(8,128)(2,1)} %bitcast.12, bf16[32768,128]{1,0:T(8,128)(2,1)} %bitcast.9, s32[1,256]{1,0:T(1,128)} %jac_state.1, ...), custom_call_target="tpu_custom_call" | custom-call | tf_op jit(solution)/shard_map/dual_space/pallas_call | solution.py:402
  24.1 1.8 %hand_over.1 = bf16[2048,128]{1,0:T(8,128)(2,1)} custom-call(bf16[2048,128]{1,0:T(8,128)(2,1)} %dual_space.1.held), custom_call_target="tpu_custom_call" | custom-call | tf_op jit(solution)/shard_map/hand_over/pallas_call | solution.py:456

commit v4 on v3

--- a/solution.py
+++ b/solution.py
@@ -10,6 +10,7 @@
 MESH = pl.DeviceIdType.MESH
 GROUP = 16
 CHUNKS = 4
+PARTS = 8
 
 
 def kernel(
@@ -26,19 +27,18 @@
     corr_row,
     corr_col,
     coupling_ref,
-    out_hbm,
+    portion,
+    picker_hbm,
     values_ref,
     weight_ref,
     picks,
-    out_ref,
     jac,
     corr,
     picker,
     weighted,
-    keeping,
     partial,
     arrived,
-    portion,
+    image,
     merged,
     state,
     coupled,
@@ -48,7 +48,8 @@
     spatial_recv,
     coupling_recv,
     obs_sem,
-    out_sem,
+    picker_sem,
+    own_sem,
     jac_sem,
     corr_sem,
     sum_send,
@@ -107,7 +108,6 @@
     def weigh(row, carry):
         rows = pl.ds(pl.multiple_of(row * width, width), width)
         keep = (lane.astype(f32) < upright(count_ref, row)).astype(f32)
-        keeping[rows, :] = keep.astype(bf16)
         weighted[rows, :] = (
             values_ref[rows, :].astype(f32) * weight_ref[rows, :].astype(f32) * keep
         ).astype(bf16)
@@ -199,7 +199,14 @@
                 ).astype(bf16)
         return carry
 
+    half = obs_rows // 2 * width
+
+    def picker_copy(part):
+        rows = pl.ds(part * half, half)
+        return pltpu.make_async_copy(picker.at[rows], picker_hbm.at[rows], picker_sem.at[part])
+
     lax.fori_loop(0, obs_rows // 2, pick_rows, 0, unroll=2)
+    picker_copy(0).start()
 
     for step, copy in sum_copies:
         copy.wait_recv()
@@ -254,6 +261,7 @@
         spatial_copy(1, now - 1).start()
 
     lax.fori_loop(obs_rows // 2, obs_rows, pick_rows, 0, unroll=2)
+    picker_copy(1).start()
 
     @pl.when(has_earlier)
     def _():
@@ -305,9 +313,7 @@
         own = every[:, :width]
         for k in range(1, GROUP):
             own = jnp.where(group_ids == k, every[:, k * width : (k + 1) * width], own)
-        portion[pl.ds(pl.multiple_of(me * jac_total + group * GROUP, GROUP), GROUP), :] = (
-            own.astype(bf16)
-        )
+        image[pl.ds(first, GROUP), :] = own.astype(bf16)
         return carry
 
     image_part = jac_total // CHUNKS
@@ -316,7 +322,7 @@
     def image_copy(part, step):
         rows = pl.ds(pl.multiple_of(me * jac_total + part * image_part, image_part), image_part)
         return pltpu.make_async_remote_copy(
-            src_ref=portion.at[rows],
+            src_ref=image.at[pl.ds(part * image_part, image_part)],
             dst_ref=portion.at[rows],
             send_sem=image_send.at[part, step - 1],
             recv_sem=image_recv.at[part, step - 1],
@@ -328,22 +334,17 @@
         lax.fori_loop(part * groups, (part + 1) * groups, images, 0, unroll=True)
         for step in range(1, tiles):
             image_copy(part, step).start()
+    own_copy = pltpu.make_async_copy(
+        image, portion.at[pl.ds(pl.multiple_of(me * jac_total, jac_total), jac_total)], own_sem
+    )
+    own_copy.start()
     for part in range(CHUNKS):
         for step in range(1, tiles):
             image_copy(part, step).wait_recv()
-
-    out_rows = obs_rows * width // CHUNKS
-    out_copies = []
-    for part in range(CHUNKS):
-        rows = pl.ds(part * out_rows, out_rows)
-        gathered = jnp.dot(picker[rows, :], portion[...], preferred_element_type=f32)
-        out_ref[rows, :] = (gathered * keeping[rows, :].astype(f32)).astype(bf16)
-        copy = pltpu.make_async_copy(out_ref.at[rows], out_hbm.at[rows], out_sem.at[part])
-        copy.start()
-        out_copies.append(copy)
-    for copy in out_copies:
-        copy.wait()
-
+    own_copy.wait()
+
+    picker_copy(0).wait()
+    picker_copy(1).wait()
     for step, copy in sum_copies:
         copy.wait_send()
     for part in range(CHUNKS):
@@ -360,16 +361,43 @@
         coupling_copy().wait_send()
 
 
-def hand_over(held, out, stage, in_sem, out_sem):
-    part = held.shape[0] // CHUNKS
+def gather(
+    count_ref,
+    portion_hbm,
+    picker_hbm,
+    out_hbm,
+    portion,
+    picker,
+    keeping,
+    out_ref,
+    portion_sem,
+    in_sem,
+    out_sem,
+):
+    f32, bf16 = jnp.float32, jnp.bfloat16
+    width = out_ref.shape[1]
+    part = out_ref.shape[0] // PARTS
+    portion_copy = pltpu.make_async_copy(portion_hbm, portion, portion_sem)
+    portion_copy.start()
     incoming, outgoing = [], []
-    for k in range(CHUNKS):
+    for k in range(PARTS):
         rows = pl.ds(k * part, part)
-        incoming.append(pltpu.make_async_copy(held.at[rows], stage.at[rows], in_sem.at[k]))
-        outgoing.append(pltpu.make_async_copy(stage.at[rows], out.at[rows], out_sem.at[k]))
+        incoming.append(pltpu.make_async_copy(picker_hbm.at[rows], picker.at[rows], in_sem.at[k]))
+        outgoing.append(pltpu.make_async_copy(out_ref.at[rows], out_hbm.at[rows], out_sem.at[k]))
         incoming[-1].start()
-    for k in range(CHUNKS):
+    lane = lax.broadcasted_iota(jnp.int32, (width, width), 1)
+    eye = lax.broadcasted_iota(jnp.int32, (width, width), 0) == lane
+    ones = jnp.ones((width, width), bf16)
+    for row in range(count_ref.shape[0]):
+        spread = jnp.where(eye, count_ref[row : row + 1, :].astype(f32), 0.0).astype(bf16)
+        count = jnp.dot(spread, ones, preferred_element_type=f32)
+        keeping[row * width : (row + 1) * width, :] = (lane.astype(f32) < count).astype(f32)
+    portion_copy.wait()
+    for k in range(PARTS):
+        rows = pl.ds(k * part, part)
         incoming[k].wait()
+        gathered = jnp.dot(picker[rows, :], portion[...], preferred_element_type=f32)
+        out_ref[rows, :] = (gathered * keeping[rows, :]).astype(bf16)
         outgoing[k].start()
     for copy in outgoing:
         copy.wait()
@@ -399,24 +427,25 @@
     smem = pl.BlockSpec(memory_space=pltpu.SMEM)
     hbm = pl.BlockSpec(memory_space=pl.ANY)
     dma = pltpu.SemaphoreType.DMA
-    out = pl.pallas_call(
+    portion, picker = pl.pallas_call(
         functools.partial(kernel, tiles, windows),
-        out_shape=jax.ShapeDtypeStruct((obs_total, width), bf16),
+        out_shape=(
+            jax.ShapeDtypeStruct((tiles * jac_total, width), bf16),
+            jax.ShapeDtypeStruct((obs_total, tiles * jac_total), bf16),
+        ),
         in_specs=[vmem] * 3 + [hbm] * 3 + [smem, hbm, smem, smem, vmem],
-        out_specs=hbm,
+        out_specs=(hbm, hbm),
         scratch_shapes=[
             pltpu.VMEM((obs_total, width), bf16),
             pltpu.VMEM((obs_total, width), bf16),
             pltpu.VMEM((2, jac_total, obs_total), bf16),
-            pltpu.VMEM((obs_total, width), bf16),
             pltpu.VMEM((jac_total * width, width), bf16),
             pltpu.VMEM((corr_total * width, width), bf16),
             pltpu.VMEM((obs_total, tiles * jac_total), bf16),
             pltpu.VMEM((obs_total, width), bf16),
-            pltpu.VMEM((obs_total, width), bf16),
             pltpu.VMEM((tiles - 1, jac_total, width), bf16),
             pltpu.VMEM((tiles - 1, jac_total, width), bf16),
-            pltpu.VMEM((tiles * jac_total, width), bf16),
+            pltpu.VMEM((jac_total, width), bf16),
             pltpu.VMEM((jac_total, width), f32),
             pltpu.VMEM((state_total, width), f32),
             pltpu.VMEM((state_total, width), f32),
@@ -426,7 +455,8 @@
             pltpu.VMEM((2, state_total, width), bf16),
             pltpu.VMEM((state_total, width), bf16),
             dma((2,)),
-            dma((CHUNKS,)),
+            dma((2,)),
+            dma,
             dma((CHUNKS,)),
             dma,
             dma((tiles - 1,)),
@@ -454,17 +484,22 @@
         time_coupling[0],
     )
     out = pl.pallas_call(
-        hand_over,
+        gather,
         out_shape=jax.ShapeDtypeStruct((obs_total, width), bf16),
-        in_specs=[hbm],
+        in_specs=[vmem, hbm, hbm],
         out_specs=hbm,
         scratch_shapes=[
+            pltpu.VMEM((tiles * jac_total, width), bf16),
+            pltpu.VMEM((obs_total, tiles * jac_total), bf16),
+            pltpu.VMEM((obs_total, width), f32),
             pltpu.VMEM((obs_total, width), bf16),
-            dma((CHUNKS,)),
-            dma((CHUNKS,)),
+            dma,
+            dma((PARTS,)),
+            dma((PARTS,)),
         ],
-        name="hand_over",
-    )(out)
+        compiler_params=pltpu.CompilerParams(vmem_limit_bytes=56 * 1024 * 1024),
+        name="gather",
+    )(obs_count.reshape(obs_total // width, width), portion, picker)
     return out[None]
 
 

time: 26.1 us -> 28.3 us (1.084)
  Pallas kernels: 25.9 us -> 28 us
    pallas_call x2, Pallas kernels: 25.9 us -> 28 us  [the longest x1 22.2 us: shards(): pl.pallas_call(functools.partial(kernel, tiles, windows), out_shape=(jax....]
where the time goes in v4:
time: 28.3 us; the launch traced here: 28.1 us
  Pallas kernels  28 us (99%)
    pallas_call x1, Pallas kernels, shards(): pl.pallas_call(functools.partial(kernel, tiles, windows), out_shape=(jax....  22.2 us
    pallas_call x1, Pallas kernels, shards(): pl.pallas_call(gather, out_shape=jax.ShapeDtypeStruct((obs_total, width),...  5.86 us

profile of v4, /device:TPU:1, one launch (start us, length us, event | category | flops | bytes accessed | tf_op | source)
XLA Modules:
  0.0 28.1 jit_solution(3375330865158331239)
XLA Ops:
  0.0 22.2 %dual_space.1 = (bf16[1024,128]{1,0:T(8,128)(2,1)}, bf16[2048,1024]{1,0:T(8,128)(2,1)}) custom-call(s32[16,128]{1,0:T(8,128)} %bitcast.13, s32[16,128]{1,0:T(8,128)} %bitcast.16, s32[16,128]{1,0:T(8,128)} %bitcast.17, bf16[2048,128]{1,0:T(8,128)(2,1)} %bitcast.11, bf16[2048,128]{1,0:T(8,128)(2,1)} %bitcast.12, bf16[32768,128]{1,0:T(8,128)(2,1)} %bitcast.9, ...), custom_call_target="tpu_custom_call" | custom-call | tf_op jit(solution)/shard_map/dual_space/pallas_call | solution.py:430
  22.2 5.9 %gather.1 = bf16[2048,128]{1,0:T(8,128)(2,1)} custom-call(s32[16,128]{1,0:T(8,128)} %bitcast.14, bf16[1024,128]{1,0:T(8,128)(2,1)} %get-tuple-element.7.portion_hbm, bf16[2048,1024]{1,0:T(8,128)(2,1)} %get-tuple-element.8.picker_hbm), custom_call_target="tpu_custom_call" | custom-call | tf_op jit(solution)/shard_map/gather/pallas_call | solution.py:486

commit v5 on v3

--- a/solution.py
+++ b/solution.py
@@ -30,6 +30,7 @@
     values_ref,
     weight_ref,
     picks,
+    early,
     out_ref,
     jac,
     corr,
@@ -185,18 +186,18 @@
         sum_copies.append((step, copy))
 
     lane_f = lane.astype(f32)
+    image_part = jac_total // CHUNKS
 
     def pick_rows(row, carry):
         rows = pl.ds(pl.multiple_of(row * width, width), width)
         column = upright(column_ref, row)
         target = upright(target_ref, row)
-        for tile in range(tiles):
-            wanted = jnp.where(target == float(tile), column, -1.0)
-            for part in range(jac_total // width):
-                start = tile * jac_total + part * width
-                picker[rows, start : start + width] = jnp.where(
-                    wanted == lane_f + float(part * width), 1.0, 0.0
-                ).astype(bf16)
+        part = jnp.floor(column * (1.0 / image_part))
+        wanted = column + float(image_part) * (target + float(tiles - 1) * part)
+        for start in range(0, tiles * jac_total, width):
+            picker[rows, start : start + width] = jnp.where(
+                wanted == lane_f + float(start), 1.0, 0.0
+            ).astype(bf16)
         return carry
 
     lax.fori_loop(0, obs_rows // 2, pick_rows, 0, unroll=2)
@@ -205,8 +206,6 @@
         copy.wait_recv()
         merged[...] += arrived[step - 1].astype(f32)
     merged[...] = merged[...].astype(bf16).astype(f32)
-    for copy in jac_copies:
-        copy.wait()
 
     state_ids = lax.broadcasted_iota(jnp.int32, (state_total, width), 0)
 
@@ -225,9 +224,14 @@
         )
 
     blank = jnp.zeros((state_total, width), f32)
-    state[...] = (
-        lax.fori_loop(0, jac_total // GROUP, to_state, blank, unroll=4).astype(bf16).astype(f32)
-    )
+    quarter = jac_total // GROUP // CHUNKS
+    gained = blank
+    for part in range(CHUNKS):
+        jac_copies[part].wait()
+        gained = lax.fori_loop(
+            part * quarter, (part + 1) * quarter, to_state, gained, unroll=True
+        )
+    state[...] = gained.astype(bf16).astype(f32)
     corr_copy.wait()
 
     def correlate(group, total):
@@ -305,16 +309,15 @@
         own = every[:, :width]
         for k in range(1, GROUP):
             own = jnp.where(group_ids == k, every[:, k * width : (k + 1) * width], own)
-        portion[pl.ds(pl.multiple_of(me * jac_total + group * GROUP, GROUP), GROUP), :] = (
-            own.astype(bf16)
-        )
+        part = group // groups
+        row = (part * tiles + me) * image_part + (group - part * groups) * GROUP
+        portion[pl.ds(pl.multiple_of(row, GROUP), GROUP), :] = own.astype(bf16)
         return carry
 
-    image_part = jac_total // CHUNKS
     groups = image_part // GROUP
 
     def image_copy(part, step):
-        rows = pl.ds(pl.multiple_of(me * jac_total + part * image_part, image_part), image_part)
+        rows = pl.ds(pl.multiple_of((part * tiles + me) * image_part, image_part), image_part)
         return pltpu.make_async_remote_copy(
             src_ref=portion.at[rows],
             dst_ref=portion.at[rows],
@@ -328,15 +331,24 @@
         lax.fori_loop(part * groups, (part + 1) * groups, images, 0, unroll=True)
         for step in range(1, tiles):
             image_copy(part, step).start()
-    for part in range(CHUNKS):
+    out_rows = obs_rows * width // CHUNKS
+    ready = (CHUNKS - 1) * tiles * image_part
+    for part in range(CHUNKS - 1):
         for step in range(1, tiles):
             image_copy(part, step).wait_recv()
-
-    out_rows = obs_rows * width // CHUNKS
+    for part in range(CHUNKS):
+        rows = pl.ds(part * out_rows, out_rows)
+        early[rows, :] = jnp.dot(
+            picker[rows, :ready], portion[:ready, :], preferred_element_type=f32
+        )
+    for step in range(1, tiles):
+        image_copy(CHUNKS - 1, step).wait_recv()
     out_copies = []
     for part in range(CHUNKS):
         rows = pl.ds(part * out_rows, out_rows)
-        gathered = jnp.dot(picker[rows, :], portion[...], preferred_element_type=f32)
+        gathered = early[rows, :] + jnp.dot(
+            picker[rows, ready:], portion[ready:, :], preferred_element_type=f32
+        )
         out_ref[rows, :] = (gathered * keeping[rows, :].astype(f32)).astype(bf16)
         copy = pltpu.make_async_copy(out_ref.at[rows], out_hbm.at[rows], out_sem.at[part])
         copy.start()
@@ -408,6 +420,7 @@
             pltpu.VMEM((obs_total, width), bf16),
             pltpu.VMEM((obs_total, width), bf16),
             pltpu.VMEM((2, jac_total, obs_total), bf16),
+            pltpu.VMEM((obs_total, width), f32),
             pltpu.VMEM((obs_total, width), bf16),
             pltpu.VMEM((jac_total * width, width), bf16),
             pltpu.VMEM((corr_total * width, width), bf16),

time: 26.1 us -> 25.5 us (0.977)
  Pallas kernels: 25.9 us -> 25.3 us
    pallas_call x1, Pallas kernels: 24 us -> 23.5 us  [shards(): pl.pallas_call(functools.partial(kernel, tiles, windows), out_shape=jax.S...]
where the time goes in v5:
time: 25.5 us; the launch traced here: 25.3 us
  Pallas kernels  25.3 us (99%)
    pallas_call x1, Pallas kernels, shards(): pl.pallas_call(functools.partial(kernel, tiles, windows), out_shape=jax.S...  23.5 us
    pallas_call x1, Pallas kernels, shards(): pl.pallas_call(hand_over, out_shape=jax.ShapeDtypeStruct((obs_total, widt...  1.82 us

profile of v5, /device:TPU:1, one launch (start us, length us, event | category | flops | bytes accessed | tf_op | source)
XLA Modules:
  0.0 25.3 jit_solution(8704997546897820260)
XLA Ops:
  0.0 23.5 %dual_space.1.held = bf16[2048,128]{1,0:T(8,128)(2,1)} custom-call(s32[16,128]{1,0:T(8,128)} %bitcast.14, s32[16,128]{1,0:T(8,128)} %bitcast.15, s32[16,128]{1,0:T(8,128)} %bitcast.16, bf16[2048,128]{1,0:T(8,128)(2,1)} %bitcast.11, bf16[2048,128]{1,0:T(8,128)(2,1)} %bitcast.12, bf16[32768,128]{1,0:T(8,128)(2,1)} %bitcast.9, s32[1,256]{1,0:T(1,128)} %jac_state.1, ...), custom_call_target="tpu_custom_call" | custom-call | tf_op jit(solution)/shard_map/dual_space/pallas_call | solution.py:414
  23.5 1.8 %hand_over.1 = bf16[2048,128]{1,0:T(8,128)(2,1)} custom-call(bf16[2048,128]{1,0:T(8,128)(2,1)} %dual_space.1.held), custom_call_target="tpu_custom_call" | custom-call | tf_op jit(solution)/shard_map/hand_over/pallas_call | solution.py:469
